TPU v7x, 512 devices: a whole 4x4x16 slice. The times are simulated.
512 devices in a mesh: freq: 16 (over y, x), patch: 32 (over z, core).
Axes of the slice: x: 4, y: 4, z: 16, core: 2. Of those that a mesh axis runs over, the one named last changes fastest.
Arguments:
- responses: bfloat16 [2048, 2, 2048], P('patch', None, 'freq'), may hold values from -6 to 6
- adjoints: bfloat16 [2048, 2, 2048], P('patch', None, 'freq'), may hold values from -6 to 6
- patch_shapes: bfloat16 [3072, 4, 48, 128], P('patch'), may hold values from -0.25 to 0.25
- block_lists: int32 [3072, 4], P('patch'), may hold values from 0 to 15
- block_counts: int32 [3072], P('patch'), may hold values from 1 to 4
- patch_sizes: int32 [3072], P('patch'), may hold values from 12 to 48
- owner_map: int32 [3072], P('patch'), may hold values from 0 to 3071, each once
Outputs:
- loss_gradient: float32 [3072], P('patch')
Inputs may be any that keep to these rules, and one draw needn't show every extreme that they name: `owner_map`: each patch appears once.
All inputs are finite; a program needn't handle non-finite values.
Results may differ from a plain program's by a relative error of at most 0.0003.
Values may be sent and summed in bfloat16 or wider, within the bound.
A program may use at most 64 MiB of HBM per device.

v0:
```python
import math
import jax
import jax.numpy as jnp
from jax import lax
from jax.sharding import PartitionSpec as P


def strain_terms(total, masked, blocks, resp_piece, adjo_piece, width):
    count = resp_piece.shape[0]
    modes = resp_piece.shape[2]
    patches = masked.shape[0]
    samples = masked.shape[2]
    step = math.gcd(count, 32)
    turns = count // step

    def one(index, carry):
        resp = lax.dynamic_slice_in_dim(resp_piece, index * step, step, 0).reshape(
            step * 2, modes // width, width
        )
        adjo = lax.dynamic_slice_in_dim(adjo_piece, index * step, step, 0).reshape(
            step * 2, modes // width, width
        )
        forward = jnp.einsum(
            "pksb,cpkb->cps", masked, resp[:, blocks, :], preferred_element_type=jnp.float32
        )
        backward = jnp.einsum(
            "pksb,cpkb->cps", masked, adjo[:, blocks, :], preferred_element_type=jnp.float32
        )
        forward = forward.reshape(step, 2, patches, samples)
        backward = backward.reshape(step, 2, patches, samples)
        cross = forward[:, 0] * backward[:, 1] - forward[:, 1] * backward[:, 0]
        return carry + jnp.sum(cross, axis=(0, 2))

    return lax.fori_loop(0, turns, one, total)


def body(responses, adjoints, patch_shapes, block_lists, block_counts, patch_sizes, owner_map):
    patch_dev, slots, samples, width = patch_shapes.shape
    slot_live = jnp.arange(slots, dtype=jnp.int32)[None, :] < block_counts[:, None]
    row_live = jnp.arange(samples, dtype=jnp.int32)[None, :] < patch_sizes[:, None]
    live = (slot_live[:, :, None, None] & row_live[:, None, :, None]).astype(jnp.bfloat16)
    masked = patch_shapes * live
    freqs = responses.shape[0] * lax.axis_size("patch")
    empty = jnp.zeros((patch_dev,), jnp.float32)
    regrouped = (
        lax.all_to_all(responses, "freq", split_axis=0, concat_axis=2, tiled=True),
        lax.all_to_all(adjoints, "freq", split_axis=0, concat_axis=2, tiled=True),
    )
    terms = strain_terms(
        empty,
        masked,
        block_lists,
        lax.all_gather(regrouped[0], "patch", axis=0, tiled=True),
        lax.all_gather(regrouped[1], "patch", axis=0, tiled=True),
        width,
    )
    terms = terms * (samples * freqs) ** (-0.5)
    patches = patch_dev * lax.axis_size("patch")
    columns = jnp.arange(patches, dtype=jnp.int32)
    onehot = (owner_map[:, None] == columns[None, :]).astype(jnp.float32)
    dense = jnp.dot(terms, onehot, precision=lax.Precision.HIGHEST)
    mine = lax.psum_scatter(dense, "patch", scatter_dimension=0, tiled=True)
    return lax.psum(mine, "freq")


def solution(mesh):
    placed = (
        P("patch", None, "freq"),
        P("patch", None, "freq"),
        P("patch", None, None, None),
        P("patch", None),
        P("patch"),
        P("patch"),
        P("patch"),
    )
    return jax.shard_map(body, mesh=mesh, in_specs=placed, out_specs=P("patch"), check_vma=False)
```

profile of v0, /device:TPU:32, one launch (start us, length us, event | category | flops | bytes accessed | tf_op | source)
XLA Modules:
  0.0 486.1 jit_solution(6683167722934066681)
XLA Ops:
  6.5 14.6 %all_to_all.36 = bf16[64,2,128]{2,1,0:T(2,128)(2,1)S(1)} all-to-all(bf16[64,2,128]{2,1,0:T(2,128)(2,1)} %param.9), channel_id=1, replica_groups=mesh['freq'=16,'patch'=32] {'freq'}, dimensions={0} | all-to-all | bytes 65536 | tf_op jit(solution)/shard_map/all_to_all | solution.py:46
  21.9 11.0 %all_to_all.37 = bf16[64,2,128]{2,1,0:T(2,128)(2,1)S(1)} all-to-all(bf16[64,2,128]{2,1,0:T(2,128)(2,1)} %param.10), channel_id=1, replica_groups=mesh['freq'=16,'patch'=32] {'freq'}, dimensions={0} | all-to-all | bytes 65536 | tf_op jit(solution)/shard_map/all_to_all | solution.py:47
  38.0 6.3 %broadcast_multiply_fusion = bf16[96,4,48,128]{3,2,1,0:T(8,128)(2,1)} fusion(bf16[96,4,48,128]{3,2,1,0:T(8,128)(2,1)} %param.11, bf16[96,4,48]{2,1,0:T(4,128)(2,1)S(1)} %and_convert_fusion), kind=kLoop, calls=%fused_computation.14 | loop fusion | flops 2359296 | bytes 9474048 | tf_op jit(solution)/shard_map/mul | solution.py:42
  44.3 48.6 %all-gather.3.cloned.1.call-done = bf16[128,2,2048]{2,1,0:T(2,128)(2,1)} async-done(((bf16[4,2,2048]{2,1,0:T(2,128)(2,1)}), bf16[128,2,2048]{2,1,0:T(2,128)(2,1)}) %all-gather.3.cloned.1.call-update) | async-done | bytes 1048592 | tf_op jit(solution)/shard_map/all_gather | solution.py:53
  92.8 70.0 %all-gather.5.cloned.1.call-done = bf16[128,2,2048]{2,1,0:T(2,128)(2,1)} async-done(((bf16[4,2,2048]{2,1,0:T(2,128)(2,1)}), bf16[128,2,2048]{2,1,0:T(2,128)(2,1)}) %all-gather.5.cloned.1.call-update) | async-done | bytes 1048592 | tf_op jit(solution)/shard_map/all_gather | solution.py:54
  162.8 185.3 %while.14 = (s32[]{:T(128)}, f32[96]{0:T(128)S(1)}, bf16[128,2,2048]{2,1,0:T(2,128)(2,1)}, s32[96,4]{1,0:T(8,128)S(1)}, bf16[96,4,48,128]{3,2,1,0:T(8,128)(2,1)}...) while((s32[]{:T(128)}, f32[96]{0:T(128)S(1)}, ...), condition=%wide.region_2.0_spmd.clone, body=%wide.region_0.0_spmd.clone.sunk | while | flops 604571840 | bytes 59785376 | solution.py:34
  164.6 13.3 %gather_fusion = bf16[384,64,128]{2,1,0:T(8,128)(2,1)} fusion(bf16[64,16,128]{2,0,1:T(8,128)(2,1)S(1)} %copy.39, s32[1024]{0:T(1024)S(1)} %pad_clamp_fusion.2), kind=kCustom, calls=%fused_computation.1.clone.clone.1 | custom fusion | bytes 12584448 | tf_op jit(solution)/shard_map/while/body/eval_jaxpr/gather | solution.py:27
  177.9 5.9 %convolution_bitcast_fusion.4 = f32[64,96,48]{0,2,1:T(8,128)S(1)} fusion(bf16[64,96,4,128]{3,0,2,1:T(8,128)(2,1)} %bitcast.66, bf16[96,4,48,128]{3,2,1,0:T(8,128)(2,1)} %get-tuple-element.233), kind=kOutput, calls=%fused_computation.2.clone.1 | convolution fusion | flops 301989888 | bytes 12189696 | tf_op jit(solution)/shard_map/while/body/eval_jaxpr/pksb,cpkb->cps/dot_general | solution.py:26
  183.9 1.9 copy.40
  186.0 13.3 %gather_fusion.1 = bf16[384,64,128]{2,1,0:T(8,128)(2,1)} fusion(bf16[64,16,128]{2,0,1:T(8,128)(2,1)S(1)} %copy.41, s32[1024]{0:T(1024)S(1)} %pad_clamp_fusion.2), kind=kCustom, calls=%fused_computation.clone.clone.1 | custom fusion | bytes 12584448 | tf_op jit(solution)/shard_map/while/body/eval_jaxpr/gather | solution.py:24
  199.3 5.9 %convolution_bitcast_fusion.5 = f32[64,96,48]{0,2,1:T(8,128)S(1)} fusion(bf16[64,96,4,128]{3,0,2,1:T(8,128)(2,1)} %bitcast.65, bf16[96,4,48,128]{3,2,1,0:T(8,128)(2,1)} %get-tuple-element.233), kind=kOutput, calls=%fused_computation.3.clone.1 | convolution fusion | flops 301989888 | bytes 12189696 | tf_op jit(solution)/shard_map/while/body/eval_jaxpr/pksb,cpkb->cps/dot_general | solution.py:23
  207.1 2.1 fusion.23
  210.9 13.3 %gather_fusion = bf16[384,64,128]{2,1,0:T(8,128)(2,1)} fusion(bf16[64,16,128]{2,0,1:T(8,128)(2,1)S(1)} %copy.39, s32[1024]{0:T(1024)S(1)} %pad_clamp_fusion.2), kind=kCustom, calls=%fused_computation.1.clone.clone.1 | custom fusion | bytes 12584448 | tf_op jit(solution)/shard_map/while/body/eval_jaxpr/gather | solution.py:27
  224.3 5.9 %convolution_bitcast_fusion.4 = f32[64,96,48]{0,2,1:T(8,128)S(1)} fusion(bf16[64,96,4,128]{3,0,2,1:T(8,128)(2,1)} %bitcast.66, bf16[96,4,48,128]{3,2,1,0:T(8,128)(2,1)} %get-tuple-element.233), kind=kOutput, calls=%fused_computation.2.clone.1 | convolution fusion | flops 301989888 | bytes 12189696 | tf_op jit(solution)/shard_map/while/body/eval_jaxpr/pksb,cpkb->cps/dot_general | solution.py:26
  230.2 1.9 copy.40
  232.3 13.3 %gather_fusion.1 = bf16[384,64,128]{2,1,0:T(8,128)(2,1)} fusion(bf16[64,16,128]{2,0,1:T(8,128)(2,1)S(1)} %copy.41, s32[1024]{0:T(1024)S(1)} %pad_clamp_fusion.2), kind=kCustom, calls=%fused_computation.clone.clone.1 | custom fusion | bytes 12584448 | tf_op jit(solution)/shard_map/while/body/eval_jaxpr/gather | solution.py:24
  245.6 5.9 %convolution_bitcast_fusion.5 = f32[64,96,48]{0,2,1:T(8,128)S(1)} fusion(bf16[64,96,4,128]{3,0,2,1:T(8,128)(2,1)} %bitcast.65, bf16[96,4,48,128]{3,2,1,0:T(8,128)(2,1)} %get-tuple-element.233), kind=kOutput, calls=%fused_computation.3.clone.1 | convolution fusion | flops 301989888 | bytes 12189696 | tf_op jit(solution)/shard_map/while/body/eval_jaxpr/pksb,cpkb->cps/dot_general | solution.py:23
  253.4 2.1 fusion.23
  257.3 13.3 %gather_fusion = bf16[384,64,128]{2,1,0:T(8,128)(2,1)} fusion(bf16[64,16,128]{2,0,1:T(8,128)(2,1)S(1)} %copy.39, s32[1024]{0:T(1024)S(1)} %pad_clamp_fusion.2), kind=kCustom, calls=%fused_computation.1.clone.clone.1 | custom fusion | bytes 12584448 | tf_op jit(solution)/shard_map/while/body/eval_jaxpr/gather | solution.py:27
  270.6 5.9 %convolution_bitcast_fusion.4 = f32[64,96,48]{0,2,1:T(8,128)S(1)} fusion(bf16[64,96,4,128]{3,0,2,1:T(8,128)(2,1)} %bitcast.66, bf16[96,4,48,128]{3,2,1,0:T(8,128)(2,1)} %get-tuple-element.233), kind=kOutput, calls=%fused_computation.2.clone.1 | convolution fusion | flops 301989888 | bytes 12189696 | tf_op jit(solution)/shard_map/while/body/eval_jaxpr/pksb,cpkb->cps/dot_general | solution.py:26
  276.5 1.9 copy.40
  278.6 13.3 %gather_fusion.1 = bf16[384,64,128]{2,1,0:T(8,128)(2,1)} fusion(bf16[64,16,128]{2,0,1:T(8,128)(2,1)S(1)} %copy.41, s32[1024]{0:T(1024)S(1)} %pad_clamp_fusion.2), kind=kCustom, calls=%fused_computation.clone.clone.1 | custom fusion | bytes 12584448 | tf_op jit(solution)/shard_map/while/body/eval_jaxpr/gather | solution.py:24
  291.9 5.9 %convolution_bitcast_fusion.5 = f32[64,96,48]{0,2,1:T(8,128)S(1)} fusion(bf16[64,96,4,128]{3,0,2,1:T(8,128)(2,1)} %bitcast.65, bf16[96,4,48,128]{3,2,1,0:T(8,128)(2,1)} %get-tuple-element.233), kind=kOutput, calls=%fused_computation.3.clone.1 | convolution fusion | flops 301989888 | bytes 12189696 | tf_op jit(solution)/shard_map/while/body/eval_jaxpr/pksb,cpkb->cps/dot_general | solution.py:23
  299.7 2.1 fusion.23
  303.6 13.3 %gather_fusion = bf16[384,64,128]{2,1,0:T(8,128)(2,1)} fusion(bf16[64,16,128]{2,0,1:T(8,128)(2,1)S(1)} %copy.39, s32[1024]{0:T(1024)S(1)} %pad_clamp_fusion.2), kind=kCustom, calls=%fused_computation.1.clone.clone.1 | custom fusion | bytes 12584448 | tf_op jit(solution)/shard_map/while/body/eval_jaxpr/gather | solution.py:27
  316.9 5.9 %convolution_bitcast_fusion.4 = f32[64,96,48]{0,2,1:T(8,128)S(1)} fusion(bf16[64,96,4,128]{3,0,2,1:T(8,128)(2,1)} %bitcast.66, bf16[96,4,48,128]{3,2,1,0:T(8,128)(2,1)} %get-tuple-element.233), kind=kOutput, calls=%fused_computation.2.clone.1 | convolution fusion | flops 301989888 | bytes 12189696 | tf_op jit(solution)/shard_map/while/body/eval_jaxpr/pksb,cpkb->cps/dot_general | solution.py:26
  322.8 1.9 copy.40
  325.0 13.3 %gather_fusion.1 = bf16[384,64,128]{2,1,0:T(8,128)(2,1)} fusion(bf16[64,16,128]{2,0,1:T(8,128)(2,1)S(1)} %copy.41, s32[1024]{0:T(1024)S(1)} %pad_clamp_fusion.2), kind=kCustom, calls=%fused_computation.clone.clone.1 | custom fusion | bytes 12584448 | tf_op jit(solution)/shard_map/while/body/eval_jaxpr/gather | solution.py:24
  338.3 5.9 %convolution_bitcast_fusion.5 = f32[64,96,48]{0,2,1:T(8,128)S(1)} fusion(bf16[64,96,4,128]{3,0,2,1:T(8,128)(2,1)} %bitcast.65, bf16[96,4,48,128]{3,2,1,0:T(8,128)(2,1)} %get-tuple-element.233), kind=kOutput, calls=%fused_computation.3.clone.1 | convolution fusion | flops 301989888 | bytes 12189696 | tf_op jit(solution)/shard_map/while/body/eval_jaxpr/pksb,cpkb->cps/dot_general | solution.py:23
  346.1 2.1 fusion.23
  348.7 89.7 %all-reduce = f32[3072]{0:T(1024)S(1)} all-reduce(f32[3072]{0:T(1024)S(1)} %bitcast.73), channel_id=2, replica_groups=mesh['freq'=16,'patch'=32] {'patch'}, use_global_device_ids=true, to_apply=%region_3.0.clone | all-reduce | flops 3072 | bytes 24576
  438.5 40.8 %psum.7 = f32[96]{0:T(128)} all-reduce(f32[96]{0:T(128)S(1)} %dynamic-slice.1), channel_id=1, replica_groups=mesh['freq'=16,'patch'=32] {'freq'}, use_global_device_ids=true, to_apply=%region_4.0 | all-reduce | flops 96 | bytes 768 | tf_op jit(solution)/shard_map/psum | solution.py:63
  (58 shorter events, 21.1 us)
Async XLA Ops:
  6.5 86.3 %all-gather.3.cloned.1.call-start = ((), (), s32[]{:S(2)}) async-start(), calls=%async_computation.2 | async-start | bytes 1081344 | tf_op jit(solution)/shard_map/all_gather | solution.py:53
  21.8 141.0 %all-gather.5.cloned.1.call-start = ((), (), s32[]{:S(2)}) async-start(), calls=%async_computation.3 | async-start | bytes 1081344 | tf_op jit(solution)/shard_map/all_gather | solution.py:54
  162.8 185.3 %copy-start = (s32[96]{0:T(128)S(1)}, s32[96]{0:T(128)}, u32[]{:S(2)}) copy-start(s32[96]{0:T(128)} %param.15) | copy-start | bytes 1156
Sparse Core Ops, SparseCore 0:
  22.0 70.8 all-gather.2
  95.0 67.8 all-gather.4
where the time goes:
time: 487 us; the launch traced here: 486 us
  blocking collectives  156 us (32%)
  local copies, waits for them, and re-layouts  133 us (27%)
  waiting for transfers between devices  119 us (24%)
  matrix products  47.9 us (10%)
  other arithmetic  16.3 us (3%)
  between operations  14.1 us (3%)
    unnamed x1, blocking collectives  89.7 us
    all_gather x1, waiting for transfers between devices, body(): lax.all_gather(regrouped[1], 'patch', axis=0, tiled=True)  70 us
    gather x4, local copies, waits for them, and re-layouts, one(): adjo[:, blocks, :]  53.2 us
    gather x4, local copies, waits for them, and re-layouts, one(): resp[:, blocks, :]  53.2 us
    all_gather x1, waiting for transfers between devices, body(): lax.all_gather(regrouped[0], 'patch', axis=0, tiled=True)  48.6 us
    psum x1, blocking collectives, body(): return lax.psum(mine, 'freq')  40.8 us
    dot_general x4, matrix products, one(): jnp.einsum('pksb,cpkb->cps', masked, adjo[:, blocks, :], preferred_elemen...  23.7 us
    dot_general x4, matrix products, one(): jnp.einsum('pksb,cpkb->cps', masked, resp[:, blocks, :], preferred_elemen...  23.7 us
  transfers between devices with their start and end apart: 2, of which 2 were waited for; matrix products, arithmetic and copies ran while one was open for 2% of the time, Pallas kernels for 0%

commit v1 on v0

--- a/solution.py
+++ b/solution.py
@@ -51,7 +51,10 @@
         masked,
         block_lists,
         lax.all_gather(regrouped[0], "patch", axis=0, tiled=True),
-        lax.all_gather(regrouped[1], "patch", axis=0, tiled=True),
+        jnp.concatenate(
+            lax.all_to_all(jnp.stack([regrouped[1]] * lax.axis_size("patch")), "patch", 0, 0),
+            axis=0,
+        ),
         width,
     )
     terms = terms * (samples * freqs) ** (-0.5)

time: 487 us -> 453 us (0.930)
  the two profiles are of different devices: /device:TPU:32 before, /device:TPU:2 now
where the time goes in v1:
time: 453 us; the launch traced here: 452 us
  blocking collectives  146 us (32%)
  local copies, waits for them, and re-layouts  134 us (30%)
  waiting for transfers between devices  75.8 us (17%)
  matrix products  47.9 us (11%)
  starting transfers between devices  18.6 us (4%)
  other arithmetic  16.3 us (4%)
  between operations  14 us (3%)
    unnamed x1, blocking collectives  93.3 us
    all_gather x1, waiting for transfers between devices, body(): lax.all_gather(regrouped[0], 'patch', axis=0, tiled=True)  69.5 us
    gather x4, local copies, waits for them, and re-layouts, one(): adjo[:, blocks, :]  53.2 us
    gather x4, local copies, waits for them, and re-layouts, one(): resp[:, blocks, :]  53.2 us
    psum x1, blocking collectives, body(): return lax.psum(mine, 'freq')  37 us
    dot_general x4, matrix products, one(): jnp.einsum('pksb,cpkb->cps', masked, adjo[:, blocks, :], preferred_elemen...  23.7 us
    dot_general x4, matrix products, one(): jnp.einsum('pksb,cpkb->cps', masked, resp[:, blocks, :], preferred_elemen...  23.7 us
    all_to_all x1, blocking collectives, body(): lax.all_to_all(adjoints, 'freq', split_axis=0, concat_axis=2, tiled=True)  15.5 us
  transfers between devices with their start and end apart: 3, of which 2 were waited for; matrix products, arithmetic and copies ran while one was open for 2% of the time, Pallas kernels for 0%

profile of v1, /device:TPU:2, one launch (start us, length us, event | category | flops | bytes accessed | tf_op | source)
XLA Modules:
  0.0 452.4 jit_solution(2360980050922202536)
XLA Ops:
  6.5 15.5 %all_to_all.38 = bf16[64,2,128]{2,1,0:T(2,128)(2,1)S(1)} all-to-all(bf16[64,2,128]{2,1,0:T(2,128)(2,1)} %param.10), channel_id=1, replica_groups=mesh['freq'=16,'patch'=32] {'freq'}, dimensions={0} | all-to-all | bytes 65536 | tf_op jit(solution)/shard_map/all_to_all | solution.py:47
  22.0 4.7 %all-to-all-start = ((bf16[64,2,128]{2,1,0:T(2,128)(2,1)}), bf16[64,2,128]{2,1,0:T(2,128)(2,1)S(1)}, u32[]{:S(2)}, u32[]{:S(2)}) async-start(bf16[64,2,128]{2,1,0:T(2,128)(2,1)} %param.9), calls=%async_computation | async-start | bytes 65536 | tf_op jit(solution)/shard_map/all_to_all | solution.py:46
  26.8 6.3 %all-to-all-done = bf16[64,2,128]{2,1,0:T(2,128)(2,1)S(1)} async-done(((bf16[64,2,128]{2,1,0:T(2,128)(2,1)}), bf16[64,2,128]{2,1,0:T(2,128)(2,1)S(1)}, u32[]{:S(2)}, u32[]{:S(2)}) %all-to-all-start) | async-done | bytes 32800 | tf_op jit(solution)/shard_map/all_to_all | solution.py:46
  33.1 1.9 stack.5
  35.0 13.8 %all-to-all-start.2 = ((bf16[32,4,2,2048]{3,2,1,0:T(2,128)(2,1)}), bf16[32,4,2,2048]{3,2,1,0:T(2,128)(2,1)}, u32[]{:S(2)}, u32[]{:S(2)}) async-start(bf16[32,4,2,2048]{3,2,1,0:T(2,128)(2,1)} %stack.5), calls=%async_computation.2 | async-start | bytes 2097152 | tf_op jit(solution)/shard_map/all_to_all | solution.py:55
  53.9 6.3 %broadcast_multiply_fusion = bf16[96,4,48,128]{3,2,1,0:T(8,128)(2,1)} fusion(bf16[96,4,48,128]{3,2,1,0:T(8,128)(2,1)} %param.11, bf16[96,4,48]{2,1,0:T(4,128)(2,1)S(1)} %and_convert_fusion), kind=kLoop, calls=%fused_computation.14 | loop fusion | flops 2359296 | bytes 9474048 | tf_op jit(solution)/shard_map/mul | solution.py:42
  60.1 69.5 %all-gather.2.cloned.1.call-done = bf16[128,2,2048]{2,1,0:T(2,128)(2,1)} async-done(((bf16[4,2,2048]{2,1,0:T(2,128)(2,1)}), bf16[128,2,2048]{2,1,0:T(2,128)(2,1)}) %all-gather.2.cloned.1.call-update) | async-done | bytes 1048592 | tf_op jit(solution)/shard_map/all_gather | solution.py:53
  129.6 185.0 %while.14 = (s32[]{:T(128)}, f32[96]{0:T(128)S(1)}, bf16[128,2,2048]{2,1,0:T(2,128)(2,1)}, s32[96,4]{1,0:T(8,128)S(1)}, bf16[96,4,48,128]{3,2,1,0:T(8,128)(2,1)}...) while((s32[]{:T(128)}, f32[96]{0:T(128)S(1)}, ...), condition=%wide.region_2.0_spmd.clone, body=%wide.region_0.0_spmd.clone.sunk | while | flops 604571840 | bytes 59785376 | solution.py:34
  131.4 13.3 %gather_fusion = bf16[384,64,128]{2,1,0:T(8,128)(2,1)} fusion(bf16[64,16,128]{2,0,1:T(8,128)(2,1)S(1)} %copy.38, s32[1024]{0:T(1024)S(1)} %pad_clamp_fusion.2), kind=kCustom, calls=%fused_computation.1.clone.clone.1 | custom fusion | bytes 12584448 | tf_op jit(solution)/shard_map/while/body/eval_jaxpr/gather | solution.py:27
  144.7 5.9 %convolution_bitcast_fusion.4 = f32[64,96,48]{0,2,1:T(8,128)S(1)} fusion(bf16[64,96,4,128]{3,0,2,1:T(8,128)(2,1)} %bitcast.67, bf16[96,4,48,128]{3,2,1,0:T(8,128)(2,1)} %get-tuple-element.233), kind=kOutput, calls=%fused_computation.2.clone.1 | convolution fusion | flops 301989888 | bytes 12189696 | tf_op jit(solution)/shard_map/while/body/eval_jaxpr/pksb,cpkb->cps/dot_general | solution.py:26
  150.6 1.8 copy.39
  152.7 13.3 %gather_fusion.1 = bf16[384,64,128]{2,1,0:T(8,128)(2,1)} fusion(bf16[64,16,128]{2,0,1:T(8,128)(2,1)S(1)} %copy.40, s32[1024]{0:T(1024)S(1)} %pad_clamp_fusion.2), kind=kCustom, calls=%fused_computation.clone.clone.1 | custom fusion | bytes 12584448 | tf_op jit(solution)/shard_map/while/body/eval_jaxpr/gather | solution.py:24
  166.0 5.9 %convolution_bitcast_fusion.5 = f32[64,96,48]{0,2,1:T(8,128)S(1)} fusion(bf16[64,96,4,128]{3,0,2,1:T(8,128)(2,1)} %bitcast.66, bf16[96,4,48,128]{3,2,1,0:T(8,128)(2,1)} %get-tuple-element.233), kind=kOutput, calls=%fused_computation.3.clone.1 | convolution fusion | flops 301989888 | bytes 12189696 | tf_op jit(solution)/shard_map/while/body/eval_jaxpr/pksb,cpkb->cps/dot_general | solution.py:23
  173.8 2.1 fusion.23
  177.7 13.3 %gather_fusion = bf16[384,64,128]{2,1,0:T(8,128)(2,1)} fusion(bf16[64,16,128]{2,0,1:T(8,128)(2,1)S(1)} %copy.38, s32[1024]{0:T(1024)S(1)} %pad_clamp_fusion.2), kind=kCustom, calls=%fused_computation.1.clone.clone.1 | custom fusion | bytes 12584448 | tf_op jit(solution)/shard_map/while/body/eval_jaxpr/gather | solution.py:27
  191.0 5.9 %convolution_bitcast_fusion.4 = f32[64,96,48]{0,2,1:T(8,128)S(1)} fusion(bf16[64,96,4,128]{3,0,2,1:T(8,128)(2,1)} %bitcast.67, bf16[96,4,48,128]{3,2,1,0:T(8,128)(2,1)} %get-tuple-element.233), kind=kOutput, calls=%fused_computation.2.clone.1 | convolution fusion | flops 301989888 | bytes 12189696 | tf_op jit(solution)/shard_map/while/body/eval_jaxpr/pksb,cpkb->cps/dot_general | solution.py:26
  196.9 1.8 copy.39
  199.0 13.3 %gather_fusion.1 = bf16[384,64,128]{2,1,0:T(8,128)(2,1)} fusion(bf16[64,16,128]{2,0,1:T(8,128)(2,1)S(1)} %copy.40, s32[1024]{0:T(1024)S(1)} %pad_clamp_fusion.2), kind=kCustom, calls=%fused_computation.clone.clone.1 | custom fusion | bytes 12584448 | tf_op jit(solution)/shard_map/while/body/eval_jaxpr/gather | solution.py:24
  212.3 5.9 %convolution_bitcast_fusion.5 = f32[64,96,48]{0,2,1:T(8,128)S(1)} fusion(bf16[64,96,4,128]{3,0,2,1:T(8,128)(2,1)} %bitcast.66, bf16[96,4,48,128]{3,2,1,0:T(8,128)(2,1)} %get-tuple-element.233), kind=kOutput, calls=%fused_computation.3.clone.1 | convolution fusion | flops 301989888 | bytes 12189696 | tf_op jit(solution)/shard_map/while/body/eval_jaxpr/pksb,cpkb->cps/dot_general | solution.py:23
  220.1 2.1 fusion.23
  223.9 13.3 %gather_fusion = bf16[384,64,128]{2,1,0:T(8,128)(2,1)} fusion(bf16[64,16,128]{2,0,1:T(8,128)(2,1)S(1)} %copy.38, s32[1024]{0:T(1024)S(1)} %pad_clamp_fusion.2), kind=kCustom, calls=%fused_computation.1.clone.clone.1 | custom fusion | bytes 12584448 | tf_op jit(solution)/shard_map/while/body/eval_jaxpr/gather | solution.py:27
  237.2 5.9 %convolution_bitcast_fusion.4 = f32[64,96,48]{0,2,1:T(8,128)S(1)} fusion(bf16[64,96,4,128]{3,0,2,1:T(8,128)(2,1)} %bitcast.67, bf16[96,4,48,128]{3,2,1,0:T(8,128)(2,1)} %get-tuple-element.233), kind=kOutput, calls=%fused_computation.2.clone.1 | convolution fusion | flops 301989888 | bytes 12189696 | tf_op jit(solution)/shard_map/while/body/eval_jaxpr/pksb,cpkb->cps/dot_general | solution.py:26
  245.3 13.3 %gather_fusion.1 = bf16[384,64,128]{2,1,0:T(8,128)(2,1)} fusion(bf16[64,16,128]{2,0,1:T(8,128)(2,1)S(1)} %copy.40, s32[1024]{0:T(1024)S(1)} %pad_clamp_fusion.2), kind=kCustom, calls=%fused_computation.clone.clone.1 | custom fusion | bytes 12584448 | tf_op jit(solution)/shard_map/while/body/eval_jaxpr/gather | solution.py:24
  258.6 5.9 %convolution_bitcast_fusion.5 = f32[64,96,48]{0,2,1:T(8,128)S(1)} fusion(bf16[64,96,4,128]{3,0,2,1:T(8,128)(2,1)} %bitcast.66, bf16[96,4,48,128]{3,2,1,0:T(8,128)(2,1)} %get-tuple-element.233), kind=kOutput, calls=%fused_computation.3.clone.1 | convolution fusion | flops 301989888 | bytes 12189696 | tf_op jit(solution)/shard_map/while/body/eval_jaxpr/pksb,cpkb->cps/dot_general | solution.py:23
  266.3 2.1 fusion.23
  270.2 13.3 %gather_fusion = bf16[384,64,128]{2,1,0:T(8,128)(2,1)} fusion(bf16[64,16,128]{2,0,1:T(8,128)(2,1)S(1)} %copy.38, s32[1024]{0:T(1024)S(1)} %pad_clamp_fusion.2), kind=kCustom, calls=%fused_computation.1.clone.clone.1 | custom fusion | bytes 12584448 | tf_op jit(solution)/shard_map/while/body/eval_jaxpr/gather | solution.py:27
  283.5 5.9 %convolution_bitcast_fusion.4 = f32[64,96,48]{0,2,1:T(8,128)S(1)} fusion(bf16[64,96,4,128]{3,0,2,1:T(8,128)(2,1)} %bitcast.67, bf16[96,4,48,128]{3,2,1,0:T(8,128)(2,1)} %get-tuple-element.233), kind=kOutput, calls=%fused_computation.2.clone.1 | convolution fusion | flops 301989888 | bytes 12189696 | tf_op jit(solution)/shard_map/while/body/eval_jaxpr/pksb,cpkb->cps/dot_general | solution.py:26
  291.5 13.3 %gather_fusion.1 = bf16[384,64,128]{2,1,0:T(8,128)(2,1)} fusion(bf16[64,16,128]{2,0,1:T(8,128)(2,1)S(1)} %copy.40, s32[1024]{0:T(1024)S(1)} %pad_clamp_fusion.2), kind=kCustom, calls=%fused_computation.clone.clone.1 | custom fusion | bytes 12584448 | tf_op jit(solution)/shard_map/while/body/eval_jaxpr/gather | solution.py:24
  304.8 5.9 %convolution_bitcast_fusion.5 = f32[64,96,48]{0,2,1:T(8,128)S(1)} fusion(bf16[64,96,4,128]{3,0,2,1:T(8,128)(2,1)} %bitcast.66, bf16[96,4,48,128]{3,2,1,0:T(8,128)(2,1)} %get-tuple-element.233), kind=kOutput, calls=%fused_computation.3.clone.1 | convolution fusion | flops 301989888 | bytes 12189696 | tf_op jit(solution)/shard_map/while/body/eval_jaxpr/pksb,cpkb->cps/dot_general | solution.py:23
  312.6 2.1 fusion.23
  315.2 93.3 %all-reduce = f32[3072]{0:T(1024)S(1)} all-reduce(f32[3072]{0:T(1024)S(1)} %bitcast.74), channel_id=2, replica_groups=mesh['freq'=16,'patch'=32] {'patch'}, use_global_device_ids=true, to_apply=%region_3.0.clone | all-reduce | flops 3072 | bytes 24576
  408.6 37.0 %psum.7 = f32[96]{0:T(128)} all-reduce(f32[96]{0:T(128)S(1)} %dynamic-slice.1), channel_id=1, replica_groups=mesh['freq'=16,'patch'=32] {'freq'}, use_global_device_ids=true, to_apply=%region_4.0 | all-reduce | flops 96 | bytes 768 | tf_op jit(solution)/shard_map/psum | solution.py:66
  (59 shorter events, 24.1 us)
Async XLA Ops:
  22.0 11.0 %all-to-all-start = ((bf16[64,2,128]{2,1,0:T(2,128)(2,1)}), bf16[64,2,128]{2,1,0:T(2,128)(2,1)S(1)}, u32[]{:S(2)}, u32[]{:S(2)}) async-start(bf16[64,2,128]{2,1,0:T(2,128)(2,1)} %param.9), calls=%async_computation | async-start | bytes 65536 | tf_op jit(solution)/shard_map/all_to_all | solution.py:46
  35.0 94.6 %all-to-all-start.2 = ((bf16[32,4,2,2048]{3,2,1,0:T(2,128)(2,1)}), bf16[32,4,2,2048]{3,2,1,0:T(2,128)(2,1)}, u32[]{:S(2)}, u32[]{:S(2)}) async-start(bf16[32,4,2,2048]{3,2,1,0:T(2,128)(2,1)} %stack.5), calls=%async_computation.2 | async-start | bytes 2097152 | tf_op jit(solution)/shard_map/all_to_all | solution.py:55
  48.8 80.8 %all-gather.2.cloned.1.call-start = ((), (), s32[]{:S(2)}) async-start(), calls=%async_computation.3 | async-start | bytes 1081344 | tf_op jit(solution)/shard_map/all_gather | solution.py:53
  129.6 185.1 %copy-start = (s32[96]{0:T(128)S(1)}, s32[96]{0:T(128)}, u32[]{:S(2)}) copy-start(s32[96]{0:T(128)} %param.15) | copy-start | bytes 1156
Sparse Core Ops, SparseCore 0:
  51.8 77.7 all-gather.1
